TPU v7x, 32 devices: a whole 2x2x4 slice. The times are simulated.
32 devices in a mesh: seq: 4 (over x, core), head: 8 (over z, y).
Axes of the slice: x: 2, y: 2, z: 4, core: 2. Of those that a mesh axis runs over, the one named last changes fastest.
Arguments:
- moe_input: bfloat16 [4096, 1536], P(('seq', 'head')), may hold values from -6 to 6
- out_grad: bfloat16 [4096, 1536], P(('seq', 'head')), may hold values from -6 to 6
- route_ids: int32 [4096, 6], P(('seq', 'head')), may hold values from 0 to 63, all different within a row; in each aligned block of 128 rows (0 to 127, 128 to 255, ...) at most 16 rows name the same one
- route_gates: float32 [4096, 6], P(('seq', 'head')), may hold values from 0.05 to 0.35
- gate_halves: bfloat16 [128, 1536, 256], P(('seq', 'head')), may hold values from -0.15625 to 0.15625
- up_halves: bfloat16 [128, 1536, 256], P(('seq', 'head')), may hold values from -0.15625 to 0.15625
- down_halves: bfloat16 [128, 256, 1536], P(('seq', 'head')), may hold values from -0.25 to 0.25
- out_proj: bfloat16 [3072, 1536], P('head'), may hold values from -0.109375 to 0.109375
- ssd_x: float32 [4096, 3072], P('seq', 'head'), may hold values from -0.125 to 0.125
- b_proj: float32 [4096, 128], P('seq'), may hold values from -0.5 to 0.5
- c_proj: float32 [4096, 128], P('seq'), may hold values from -0.5 to 0.5
- log_decay: float32 [48, 4096], P('head', 'seq'), may hold values from -2.3 to 0, as said below
- skip_gain: float32 [48], P('head'), may hold values from 0.5 to 1.5
Outputs:
- resid_grad: bfloat16 [4096, 1536], P(('seq', 'head'))
- ssd_x_grad: float32 [4096, 3072], P('seq', 'head')
- b_grad: float32 [4096, 128], P(('seq', 'head'))
Inputs may be any that keep to these rules, and one draw needn't show every extreme that they name: `route_ids`: each row names 6 different experts; the 128 rows of one device name any one expert at most 16 times, a bound that some block reaches. `log_decay`: negative.
All inputs are finite; a program needn't handle non-finite values.
Results may differ from a plain program's by a relative error of at most 0.0039.
Values may be sent and summed in bfloat16 or wider, within the bound.
A program may use at most 128 MiB of HBM per device.

v0:
```python
import jax
import jax.numpy as jnp
from jax import lax
from jax.sharding import PartitionSpec as P

BLOCK = 256


def from_partner(shard, axis, distance):
    return lax.ppermute(shard, axis, [(i, i ^ 1 << distance) for i in range(lax.axis_size(axis))])


def entering(part, axis, combine, identity):
    count = lax.axis_size(axis)
    place = lax.axis_index(axis)
    ahead = count - 1 - place
    gathered = jax.tree.map(lambda a: lax.all_gather(a, axis), part)
    state = jax.tree.map(lambda a, e: jnp.zeros_like(a) + jnp.asarray(e, a.dtype), part, identity)

    def one(lap, state):
        source = count - 1 - lap
        return combine(
            state, jax.tree.map(lambda a: lax.dynamic_index_in_dim(a, source, 0, False), gathered)
        )

    return lax.fori_loop(0, ahead, one, state)


def swiglu_back(recv_input, recv_grad, gate_w, up_w, down_w):
    gate_act = jnp.einsum("shcd,hdf->shcf", recv_input, gate_w, preferred_element_type=jnp.float32)
    up_act = jnp.einsum("shcd,hdf->shcf", recv_input, up_w, preferred_element_type=jnp.float32)
    hidden_grad = jnp.einsum(
        "shcd,hfd->shcf", recv_grad, down_w, preferred_element_type=jnp.float32
    )
    sigmoid_act = jax.nn.sigmoid(gate_act)
    gate_grad = (
        hidden_grad * up_act * sigmoid_act * (1.0 + gate_act * (1.0 - sigmoid_act))
    ).astype(jnp.bfloat16)
    up_grad = (hidden_grad * gate_act * sigmoid_act).astype(jnp.bfloat16)
    result = jnp.einsum("shcf,hdf->shcd", gate_grad, gate_w, preferred_element_type=jnp.float32)
    return result + jnp.einsum("shcf,hdf->shcd", up_grad, up_w, preferred_element_type=jnp.float32)


def shards(
    moe_input,
    out_grad,
    route_ids,
    route_gates,
    gate_halves,
    up_halves,
    down_halves,
    out_proj,
    ssd_x,
    b_proj,
    c_proj,
    log_decay,
    skip_gain,
):
    highest = lax.Precision.HIGHEST
    tok_rows, feature_width = moe_input.shape
    top_count = route_ids.shape[1]
    devices = lax.axis_size(("seq", "head"))
    halves_dev = gate_halves.shape[0]
    experts = devices * halves_dev // 2
    capacity = tok_rows // 8
    flat_ids = route_ids.reshape(-1)
    onehot = (flat_ids[:, None] == jnp.arange(experts, dtype=jnp.int32)[None, :]).astype(jnp.int32)
    before = jnp.cumsum(onehot, axis=0) - onehot
    route_rank = jnp.sum(before * onehot, axis=1)
    route_slot = flat_ids * capacity + route_rank
    route_total = flat_ids.shape[0]
    filled = (
        jnp.zeros((experts * capacity,), jnp.int32)
        .at[route_slot]
        .set(jnp.arange(route_total, dtype=jnp.int32) + 1)
    )
    live_slot = filled > 0
    slot_token = jnp.maximum(filled - 1, 0) // top_count
    zero_row = jnp.zeros((), jnp.bfloat16)
    input_rows = jnp.where(live_slot[:, None], moe_input[slot_token], zero_row)
    grad_rows = jnp.where(live_slot[:, None], out_grad[slot_token], zero_row)
    half_width = gate_halves.shape[2]
    if halves_dev == 1:
        parity = lax.axis_index(("seq", "head")) % 2
        other_gate, other_up, other_down = from_partner(
            (gate_halves, up_halves, down_halves), ("seq", "head"), 0
        )
        first_side = parity == 0
        gate_w = jnp.concatenate(
            [
                jnp.where(first_side, gate_halves, other_gate),
                jnp.where(first_side, other_gate, gate_halves),
            ],
            axis=2,
        )
        up_w = jnp.concatenate(
            [
                jnp.where(first_side, up_halves, other_up),
                jnp.where(first_side, other_up, up_halves),
            ],
            axis=2,
        )
        down_w = jnp.concatenate(
            [
                jnp.where(first_side, down_halves, other_down),
                jnp.where(first_side, other_down, down_halves),
            ],
            axis=1,
        )
        items_dev = 1
    else:
        items_dev = halves_dev // 2
        gate_w = (
            gate_halves.reshape(items_dev, 2, feature_width, half_width)
            .transpose(0, 2, 1, 3)
            .reshape(items_dev, feature_width, 2 * half_width)
        )
        up_w = (
            up_halves.reshape(items_dev, 2, feature_width, half_width)
            .transpose(0, 2, 1, 3)
            .reshape(items_dev, feature_width, 2 * half_width)
        )
        down_w = down_halves.reshape(items_dev, 2 * half_width, feature_width)
    slot_count = experts * capacity // (devices * items_dev)
    send_input = input_rows.reshape(devices, items_dev, slot_count, feature_width)
    send_grad = grad_rows.reshape(devices, items_dev, slot_count, feature_width)
    recv_input = lax.all_to_all(
        send_input, ("seq", "head"), split_axis=0, concat_axis=0, tiled=True
    )
    recv_grad = lax.all_to_all(send_grad, ("seq", "head"), split_axis=0, concat_axis=0, tiled=True)
    replica_out = swiglu_back(recv_input, recv_grad, gate_w, up_w, down_w).astype(jnp.bfloat16)
    returned = lax.all_to_all(replica_out, ("seq", "head"), split_axis=0, concat_axis=0, tiled=True)
    expert_rows = returned.reshape(experts * capacity, feature_width)
    route_terms = expert_rows[route_slot].reshape(tok_rows, top_count, feature_width)
    moe_grad = jnp.sum(route_gates[:, :, None] * route_terms, axis=1)
    resid_grad = (out_grad.astype(jnp.float32) + moe_grad).astype(jnp.bfloat16)
    inner_dev = out_proj.shape[0]
    heads_dev = skip_gain.shape[0]
    head_dim = inner_dev // heads_dev
    seq_rows, state_dim = b_proj.shape
    block_len = BLOCK
    block_count = seq_rows // block_len
    decay = log_decay.reshape(heads_dev, block_count, block_len)
    within = jnp.cumsum(decay, axis=2)
    block_sum = within[:, :, -1]
    offset = jnp.cumsum(block_sum, axis=1) - block_sum
    total = offset[:, -1] + block_sum[:, -1]
    b_blocks = b_proj.reshape(block_count, block_len, state_dim)
    c_blocks = c_proj.reshape(block_count, block_len, state_dim)
    x_blocks = ssd_x.reshape(block_count, block_len, heads_dev, head_dim)
    scores = jnp.einsum("btn,bsn->bts", c_blocks, b_blocks, precision=highest)
    causal = jnp.arange(block_len)[:, None] >= jnp.arange(block_len)[None, :]
    log_gap = within[:, :, :, None] - within[:, :, None, :]
    weights = jnp.where(causal, jnp.exp(jnp.where(causal, log_gap, 0.0)), 0.0) * scores[None]
    to_start = jnp.exp(within)
    to_end = jnp.exp(block_sum[:, :, None] - within)
    block_decay = jnp.exp(block_sum)
    ssd_grad = jnp.einsum(
        "td,kd->tk",
        lax.all_gather(resid_grad, "head", axis=0, tiled=True),
        out_proj,
        preferred_element_type=jnp.float32,
    )
    g_blocks = ssd_grad.reshape(block_count, block_len, heads_dev, head_dim)
    intra_x = jnp.einsum("hbts,bthp->bshp", weights, g_blocks, precision=highest)
    inner_prod = jnp.einsum("bthp,bshp->hbts", g_blocks, x_blocks, precision=highest)
    intra_b = jnp.einsum("hbts,btn->bsn", weights * inner_prod, c_blocks, precision=highest)
    block_state = jnp.einsum("hbt,bthp,btn->bhpn", to_start, g_blocks, c_blocks, precision=highest)

    def block_step(carry, blocks_in):
        factor, summary = blocks_in
        return (factor[:, None, None] * carry + summary, carry)

    zero_state = jnp.zeros((heads_dev, head_dim, state_dim), jnp.float32)
    dev_state, future_local = lax.scan(
        block_step, zero_state, (block_decay.T, block_state), reverse=True
    )
    dev_decay = jnp.exp(total)

    def combine_pair(earlier, later):
        return (earlier[0] * later[0], later[0][:, None, None] * earlier[1] + later[1])

    identity = (jnp.ones((heads_dev,), jnp.float32), zero_state)
    incoming = entering((dev_decay, dev_state), "seq", combine_pair, identity)[1]
    tail_block = jnp.exp(total[:, None] - offset - block_sum)
    future = future_local + tail_block.T[:, :, None, None] * incoming[None]
    cross_x = jnp.einsum("hbs,bsn,bhpn->bshp", to_end, b_blocks, future, precision=highest)
    grad_x = intra_x + cross_x + skip_gain[None, None, :, None] * g_blocks
    cross_b = jnp.einsum("hbs,bshp,bhpn->bsn", to_end, x_blocks, future, precision=highest)
    partial_b = (intra_b + cross_b).reshape(seq_rows, state_dim)
    b_grad = lax.psum_scatter(partial_b, "head", scatter_dimension=0, tiled=True)
    return (resid_grad, grad_x.reshape(seq_rows, inner_dev), b_grad)


def solution(mesh):
    return jax.shard_map(
        shards,
        mesh=mesh,
        in_specs=(
            P(("seq", "head"), None),
            P(("seq", "head"), None),
            P(("seq", "head"), None),
            P(("seq", "head"), None),
            P(("seq", "head"), None, None),
            P(("seq", "head"), None, None),
            P(("seq", "head"), None, None),
            P("head", None),
            P("seq", "head"),
            P("seq", None),
            P("seq", None),
            P("head", "seq"),
            P("head"),
        ),
        out_specs=(P(("seq", "head"), None), P("seq", "head"), P(("seq", "head"), None)),
        check_vma=False,
    )
```

profile of v0, /device:TPU:0, one launch (start us, length us, event | category | flops | bytes accessed | tf_op | source)
XLA Modules:
  0.0 482.7 jit_solution(6984521763128181677)
XLA Ops:
  12.7 4.4 reduce-window.14
  21.7 3.5 scatter_custom_fusion
  25.9 5.6 %gather_fusion = bf16[1024,1536]{1,0:T(8,128)(2,1)} fusion(bf16[128,1536]{1,0:T(8,128)(2,1)S(1)} %copy-done.2, s32[1024]{0:T(1024)S(1)} %fusion.62), kind=kCustom, calls=%fused_computation | custom fusion | bytes 6295552 | tf_op jit(solution)/shard_map/gather | solution.py:81
  31.4 8.4 %gather_fusion.1 = bf16[1024,1536]{1,0:T(8,128)(2,1)} fusion(bf16[128,1536]{1,0:T(8,128)(2,1)} %param.17, s32[1024]{0:T(1024)S(1)} %fusion.62), kind=kCustom, calls=%fused_computation.1 | custom fusion | bytes 6295552 | tf_op jit(solution)/shard_map/gather | solution.py:80
  40.6 4.3 broadcast_select_fusion.1
  44.9 79.7 %all_to_all.15 = bf16[32,2,16,1536]{3,2,1,0:T(8,128)(2,1)} all-to-all(bf16[32,2,16,1536]{3,2,1,0:T(8,128)(2,1)S(1)} %get-tuple-element.241), channel_id=1, replica_groups=mesh['seq'=4,'head'=8] {'seq','head'}, dimensions={0} | all-to-all | bytes 6291456 | tf_op jit(solution)/shard_map/all_to_all | solution.py:127
  124.6 3.7 all-to-all-start
  128.3 8.0 %copy.62 = bf16[2,1536,2,256]{3,2,1,0:T(2,128)(2,1)} copy(bf16[2,1536,2,256]{3,1,2,0:T(8,128)(2,1)} %bitcast.184) | data formatting | bytes 6291456 | tf_op jit(solution)/shard_map/transpose | solution.py:115
  136.3 6.0 %reshape.232 = bf16[2,1536,512,1]{2,1,0,3:T(8,128)(2,1)} reshape(bf16[2,1536,2,256]{3,2,1,0:T(2,128)(2,1)} %copy.62) | data formatting | bytes 6291456 | tf_op jit(solution)/shard_map/reshape | solution.py:116
  142.3 8.0 %copy.60 = bf16[2,1536,2,256]{3,2,1,0:T(2,128)(2,1)} copy(bf16[2,1536,2,256]{3,1,2,0:T(8,128)(2,1)} %bitcast.185) | data formatting | bytes 6291456 | tf_op jit(solution)/shard_map/transpose | solution.py:120
  150.2 6.0 %reshape.231 = bf16[2,1536,512,1]{2,1,0,3:T(8,128)(2,1)} reshape(bf16[2,1536,2,256]{3,2,1,0:T(2,128)(2,1)} %copy.60) | data formatting | bytes 6291456 | tf_op jit(solution)/shard_map/reshape | solution.py:121
  156.3 5.9 %fusion.5 = f32[2,32,16,512]{3,2,1,0:T(8,128)} fusion(bf16[2,1536,512,1]{2,1,0,3:T(8,128)(2,1)} %reshape.232, bf16[32,2,16,1536]{3,2,1,0:T(8,128)(2,1)} %all_to_all.15), kind=kOutput, calls=%fused_computation.18 | convolution fusion | flops 1610612736 | bytes 8388608 | tf_op jit(solution)/shard_map/shcd,hdf->shcf/dot_general | solution.py:30
  162.2 39.1 %all-to-all-done = bf16[32,2,16,1536]{3,2,1,0:T(8,128)(2,1)} async-done(((bf16[32,2,16,1536]{3,2,1,0:T(8,128)(2,1)}), bf16[32,2,16,1536]{3,2,1,0:T(8,128)(2,1)}, u32[]{:S(2)}, u32[]{:S(2)}) %all-to-all-start) | async-done | bytes 3145760 | tf_op jit(solution)/shard_map/all_to_all | solution.py:130
  201.3 5.1 %fusion.10 = f32[2,32,16,512]{3,2,1,0:T(8,128)} fusion(bf16[2,512,1536,1]{2,1,3,0:T(8,128)(2,1)S(1)} %bitcast.174, bf16[32,2,16,1536]{3,2,1,0:T(8,128)(2,1)} %all-to-all-done), kind=kOutput, calls=%fused_computation.23 | convolution fusion | flops 1610612736 | bytes 8388608 | tf_op jit(solution)/shard_map/shcd,hfd->shcf/dot_general | solution.py:32
  206.3 11.5 %fusion.3 = f32[2,32,16,1536]{3,2,1,0:T(8,128)} fusion(bf16[2,1536,512,1]{2,1,0,3:T(8,128)(2,1)} %reshape.232, f32[2,32,16,512]{3,2,1,0:T(8,128)} %fusion.5, f32[2,32,16,512]{3,2,1,0:T(8,128)} %fusion.10, bf16[2,1536,512,1]{2,1,0,3:T(8,128)(2,1)} %reshape.231, bf16[32,2,16,1536]{3,2,1,0:T(8,128)(2,1)} %all_to_all.15), kind=kOutput, calls=%fused_computation.16 | convolution fusion | flops 3226468352 | bytes 19922944 | tf_op jit(solution)/shard_map/shcf,hdf->shcd/dot_general | solution.py:40
  217.8 5.9 %fusion.2 = bf16[32,2,16,1536]{3,2,0,1:T(8,128)(2,1)S(1)} fusion(f32[2,32,16,1536]{3,2,1,0:T(8,128)} %fusion.3, bf16[2,1536,512,1]{2,1,0,3:T(8,128)(2,1)S(1)} %copy-done.5, f32[2,32,16,512]{3,2,1,0:T(8,128)} %fusion.5, f32[2,32,16,512]{3,2,1,0:T(8,128)} %fusion.10), kind=kOutput, calls=%fused_computation.15 | convolution fusion | flops 1616904192 | bytes 16777216 | tf_op jit(solution)/shard_map/shcf,hdf->shcd/dot_general | solution.py:41
  225.6 2.9 all-to-all-start.2
  229.7 71.9 %all-to-all-done.2 = bf16[32,2,16,1536]{3,2,1,0:T(8,128)(2,1)S(1)} async-done(((bf16[32,2,16,1536]{3,2,1,0:T(8,128)(2,1)}), bf16[32,2,16,1536]{3,2,1,0:T(8,128)(2,1)S(1)}, u32[]{:S(2)}, u32[]{:S(2)}) %all-to-all-start.2) | async-done | bytes 3145760 | tf_op jit(solution)/shard_map/all_to_all | solution.py:132
  301.6 3.9 gather_fusion.2
  305.5 5.0 %reshape.187 = f32[128,6,1536]{2,1,0:T(8,128)} reshape(bf16[768,1536]{1,0:T(8,128)(2,1)} %gather_fusion.2) | data formatting | bytes 7077888 | tf_op jit(solution)/shard_map/convert_element_type | solution.py:135
  310.5 5.1 %multiply_reduce_fusion.1 = f32[128,1536]{1,0:T(8,128)S(1)} fusion(f32[128,6,1536]{2,1,0:T(8,128)} %reshape.187, f32[128,6]{1,0:T(8,128)S(1)} %copy-done.7), kind=kLoop, calls=%fused_computation.13 | loop fusion | flops 2162688 | bytes 5508096 | tf_op jit(solution)/shard_map/reduce_sum | solution.py:135
  316.6 7.2 %reduce-window.16 = f32[6,4,2,128]{3,2,1,0:T(2,128)S(1)} reduce-window(f32[6,4,2,128]{3,2,1,0:T(2,128)S(1)} %reshape.180, f32[]{:T(128)} %constant.117.clone.1), window={size=1x1x1x128 pad=0_0x0_0x0_0x127_0}, to_apply=%region_5.6 | reduce-window | flops 780288 | bytes 49156 | tf_op jit(solution)/shard_map/reduce-window.2
  325.9 6.5 %all-reduce = f32[24]{0:T(128)S(1)} all-reduce(f32[24]{0:T(128)S(1)} %bitcast_dynamic-update-slice_fusion.1), channel_id=2, replica_groups=mesh['seq'=4,'head'=8] {'seq'}, use_global_device_ids=true, to_apply=%add | all-reduce | flops 24 | bytes 192
  338.5 36.1 %all-gather.4.cloned.1.call-done = bf16[1024,1536]{1,0:T(8,128)(2,1)} async-done(((bf16[128,1536]{1,0:T(8,128)(2,1)}), bf16[1024,1536]{1,0:T(8,128)(2,1)}) %all-gather.4.cloned.1.call-update) | async-done | bytes 3145744 | tf_op jit(solution)/shard_map/all_gather | solution.py:160
  374.6 4.8 fusion.73
  384.2 4.3 while.32
  388.6 9.0 %all-gather.1 = f32[24,64,128]{2,1,0:T(8,128)} all-gather(f32[6,64,128]{2,1,0:T(8,128)S(1)} %get-tuple-element.192), channel_id=3, replica_groups=mesh['seq'=4,'head'=8] {'seq'}, dimensions={0}, use_global_device_ids=true | all-gather | bytes 983040 | tf_op jit(solution)/shard_map/all_gather | solution.py:17
  397.6 3.2 while.31
  400.9 9.4 %multiply_reduce_fusion = f32[4,256,256]{2,1,0:T(8,128)S(1)} fusion(f32[4,256,256]{2,1,0:T(8,128)} %fusion.74, f32[6,4,256]{2,0,1:T(8,128)S(1)} %get-tuple-element.239, pred[256,256]{1,0:T(8,128)(4,1)S(1)} %iota_compare_fusion, f32[4,256,6,64]{1,0,3,2:T(4,128)} %reshape.185, f32[4,256,6,64]{1,0,3,2:T(4,128)S(1)} %reshape.179), kind=kOutput, calls=%fused_computation.10 | convolution fusion | flops 1217134592 | bytes 5332992 | tf_op jit(solution)/shard_map/bthp,bshp->hbts/dot_general | solution.py:166
  418.4 6.8 %fusion.33 = f32[4,256,6,64]{1,3,2,0:T(8,128)S(1)} fusion(f32[4,6,64,256]{3,2,1,0:T(8,128)S(1)} %fusion.53, f32[4,256,256]{2,1,0:T(8,128)} %fusion.74, f32[6,4,256]{2,0,1:T(8,128)S(1)} %get-tuple-element.239, pred[256,256]{1,0:T(8,128)(4,1)S(1)} %iota_compare_fusion, f32[4,256,6,64]{1,0,3,2:T(4,128)S(1)} %reshape.179, f32[6]{0:T(128)S(1)} %copy-done.12, ...), kind=kOutput, calls=%fused_computation.49 | convolution fusion | flops 1215823872 | bytes 5881880 | tf_op jit(solution)/shard_map/hbts,bthp->bshp/dot_general | solution.py:165
  427.7 3.1 copy.81
  430.8 44.8 %reduce-scatter.2.cloned.1.call-done = f32[128,128]{1,0:T(8,128)} async-done(((f32[1024,128]{1,0:T(8,128)}), f32[128,128]{1,0:T(8,128)}) %reduce-scatter.2.cloned.1.call-update) | async-done | bytes 65552 | tf_op jit(solution)/shard_map/reduce_scatter | solution.py:191
  (104 shorter events, 45.6 us)
Async XLA Ops:
  7.2 194.1 %copy-start = (bf16[4,256,1536]{2,1,0:T(8,128)(2,1)S(1)}, bf16[4,256,1536]{2,1,0:T(8,128)(2,1)}, u32[]{:S(2)}) copy-start(bf16[4,256,1536]{2,1,0:T(8,128)(2,1)} %param.23) | copy-start | bytes 9437188
  7.2 18.7 %copy-start.2 = (bf16[128,1536]{1,0:T(8,128)(2,1)S(1)}, bf16[128,1536]{1,0:T(8,128)(2,1)}, u32[]{:S(2)}) copy-start(bf16[128,1536]{1,0:T(8,128)(2,1)} %param.18) | copy-start | bytes 1179652
  21.1 0.6 copy-start.9
  124.6 76.7 %all-to-all-start = ((bf16[32,2,16,1536]{3,2,1,0:T(8,128)(2,1)}), bf16[32,2,16,1536]{3,2,1,0:T(8,128)(2,1)}, u32[]{:S(2)}, u32[]{:S(2)}) async-start(bf16[32,2,16,1536]{3,2,1,0:T(8,128)(2,1)} %get-tuple-element.240), calls=%async_computation | async-start | bytes 6291456 | tf_op jit(solution)/shard_map/all_to_all | solution.py:130
  206.3 11.5 %copy-start.5 = (bf16[2,1536,512,1]{2,1,0,3:T(8,128)(2,1)S(1)}, bf16[2,1536,512,1]{2,1,0,3:T(8,128)(2,1)}, u32[]{:S(2)}) copy-start(bf16[2,1536,512,1]{2,1,0,3:T(8,128)(2,1)} %reshape.231) | copy-start | bytes 9437188
  225.6 3.4 copy-start.11
  225.6 4.1 copy-start.10
  225.6 76.0 %all-to-all-start.2 = ((bf16[32,2,16,1536]{3,2,1,0:T(8,128)(2,1)}), bf16[32,2,16,1536]{3,2,1,0:T(8,128)(2,1)S(1)}, u32[]{:S(2)}, u32[]{:S(2)}) async-start(bf16[32,2,16,1536]{3,2,1,0:T(8,128)(2,1)} %copy.64), calls=%async_computation.2 | async-start | bytes 6291456 | tf_op jit(solution)/shard_map/all_to_all | solution.py:132
  228.5 146.1 %all-gather.4.cloned.1.call-start = ((), (), s32[]{:S(2)}) async-start(), calls=%async_computation.4 | async-start | bytes 3538944 | tf_op jit(solution)/shard_map/all_gather | solution.py:160
  305.5 5.0 %copy-start.7 = (f32[128,6]{1,0:T(8,128)S(1)}, f32[128,6]{1,0:T(8,128)}, u32[]{:S(2)}) copy-start(f32[128,6]{1,0:T(8,128)} %copy.54) | copy-start | bytes 9220
  310.5 6.1 %copy-start.8 = (f32[6,1024]{1,0:T(8,128)S(1)}, f32[6,1024]{1,0:T(8,128)}, u32[]{:S(2)}) copy-start(f32[6,1024]{1,0:T(8,128)} %param.28) | copy-start | bytes 73732
  310.5 14.1 %copy-start.13 = (u32[32]{0:T(128)S(1)}, u32[32]{0:T(128)}, u32[]{:S(2)}) copy-start(u32[32]{0:T(128)} %constant.127) | copy-start | bytes 388
  316.5 159.2 %reduce-scatter.2.cloned.1.call-start = ((), (), s32[]{:S(2)}) async-start(), calls=%async_computation.5 | async-start | bytes 589824 | tf_op jit(solution)/shard_map/reduce_scatter | solution.py:191
  332.5 4.0 copy-start.4
  332.5 4.0 copy-start.6
  400.9 9.4 %copy-start.3 = (f32[4,256,6,64]{1,0,3,2:T(4,128)S(1)}, f32[4,256,6,64]{1,0,3,2:T(4,128)}, u32[]{:S(2)}) copy-start(f32[4,256,6,64]{1,0,3,2:T(4,128)} %reshape.185) | copy-start | bytes 4718596
  413.1 5.2 %copy-start.12 = (f32[6]{0:T(128)S(1)}, f32[6]{0:T(128)}, u32[]{:S(2)}) copy-start(f32[6]{0:T(128)} %param.29) | copy-start | bytes 76
  426.2 49.4 %copy-start.1 = (bf16[4,256,1536]{2,1,0:T(8,128)(2,1)S(1)}, bf16[4,256,1536]{2,1,0:T(8,128)(2,1)}, u32[]{:S(2)}) copy-start(bf16[4,256,1536]{2,1,0:T(8,128)(2,1)} %param.23) | copy-start | bytes 9437188
Sparse Core Ops, SparseCore 0:
  316.6 57.9 all-gather.3
  416.0 59.6 reduce-scatter.1
where the time goes:
time: 488 us; the launch traced here: 483 us
  waiting for transfers between devices  192 us (39%)
  blocking collectives  95.2 us (20%)
  local copies, waits for them, and re-layouts  77.5 us (16%)
  matrix products  61.9 us (13%)
  other arithmetic  33.4 us (7%)
  between operations  15.3 us (3%)
  starting transfers between devices  7.11 us (1%)
    all_to_all x1, blocking collectives, shards(): lax.all_to_all(send_input, ('seq', 'head'), split_axis=0, concat_axis=0,...  79.7 us
    all_to_all x1, waiting for transfers between devices, shards(): lax.all_to_all(replica_out, ('seq', 'head'), split_axis=0, concat_axis=0,...  71.9 us
    reduce_scatter x1, waiting for transfers between devices, shards(): lax.psum_scatter(partial_b, 'head', scatter_dimension=0, tiled=True)  44.8 us
    all_to_all x1, waiting for transfers between devices, shards(): lax.all_to_all(send_grad, ('seq', 'head'), split_axis=0, concat_axis=0, t...  39.1 us
    all_gather x1, waiting for transfers between devices, shards(): lax.all_gather(resid_grad, 'head', axis=0, tiled=True)  36.1 us
    another operation x5, other arithmetic  11.8 us
    dot_general x1, matrix products, swiglu_back(): jnp.einsum('shcf,hdf->shcd', gate_grad, gate_w, preferred_element_type=jn...  11.5 us
    unnamed x36, local copies, waits for them, and re-layouts  10.2 us
  transfers between devices with their start and end apart: 4, of which 4 were waited for; matrix products, arithmetic and copies ran while one was open for 13% of the time, Pallas kernels for 0%

commit v1 on v0

v1 whole, which is shorter than its diff:
```python
import functools
import jax
import jax.numpy as jnp
from jax import lax
from jax.experimental import pallas as pl
from jax.experimental.pallas import tpu as pltpu
from jax.sharding import PartitionSpec as P

BLOCK = 256
DEVICES = ("seq", "head")


def from_partner(shard, axis, distance):
    return lax.ppermute(shard, axis, [(i, i ^ 1 << distance) for i in range(lax.axis_size(axis))])


def expert_kernel(x_ref, g_ref, gate_ref, up_ref, down_ref, out_ref):
    last = (((1,), (1,)), ((), ()))
    f32 = jnp.float32
    x, g = x_ref[...], g_ref[...]
    total = None
    for j in range(gate_ref.shape[0]):
        gate_act = jnp.dot(x, gate_ref[j], preferred_element_type=f32)
        up_act = jnp.dot(x, up_ref[j], preferred_element_type=f32)
        hidden_grad = lax.dot_general(g, down_ref[j], last, preferred_element_type=f32)
        s = jax.nn.sigmoid(gate_act)
        gate_grad = (hidden_grad * up_act * s * (1.0 + gate_act * (1.0 - s))).astype(jnp.bfloat16)
        up_grad = (hidden_grad * gate_act * s).astype(jnp.bfloat16)
        term = lax.dot_general(gate_grad, gate_ref[j], last, preferred_element_type=f32)
        term = term + lax.dot_general(up_grad, up_ref[j], last, preferred_element_type=f32)
        total = term if total is None else total + term
    out_ref[...] = total.astype(out_ref.dtype)


def swiglu_back(rows_in, rows_grad, gate, up, down):
    rows, width = rows_in.shape
    halves, _, hidden = gate.shape
    tile = 256 if rows % 256 == 0 else rows
    row = pl.BlockSpec((tile, width), lambda i: (i, 0))
    return pl.pallas_call(
        expert_kernel,
        grid=(rows // tile,),
        in_specs=[
            row,
            row,
            pl.BlockSpec(gate.shape, lambda i: (0, 0, 0)),
            pl.BlockSpec(up.shape, lambda i: (0, 0, 0)),
            pl.BlockSpec(down.shape, lambda i: (0, 0, 0)),
        ],
        out_specs=row,
        out_shape=jax.ShapeDtypeStruct((rows, width), jnp.bfloat16),
        compiler_params=pltpu.CompilerParams(vmem_limit_bytes=48 * 1024 * 1024),
        cost_estimate=pl.CostEstimate(
            flops=10 * rows * width * halves * hidden,
            bytes_accessed=6 * rows * width + 6 * halves * width * hidden,
            transcendentals=rows * halves * hidden,
        ),
    )(rows_in, rows_grad, gate, up, down)


def split_bf16(a):
    high = a.astype(jnp.bfloat16)
    return high, (a - high.astype(jnp.float32)).astype(jnp.bfloat16)


def shards(
    moe_input,
    out_grad,
    route_ids,
    route_gates,
    gate_halves,
    up_halves,
    down_halves,
    out_proj,
    ssd_x,
    b_proj,
    c_proj,
    log_decay,
    skip_gain,
):
    highest = lax.Precision.HIGHEST
    tok_rows, feature_width = moe_input.shape
    top_count = route_ids.shape[1]
    devices = lax.axis_size(("seq", "head"))
    halves_dev = gate_halves.shape[0]
    experts = devices * halves_dev // 2
    capacity = tok_rows // 8
    expert_ids = jnp.arange(experts, dtype=jnp.int32)
    chosen = route_ids[:, :, None] == expert_ids[None, None, :]
    member = jnp.any(chosen, axis=1)
    gate_of = jnp.sum(jnp.where(chosen, route_gates[:, :, None], 0.0), axis=1)
    token = jnp.arange(tok_rows)
    earlier = (token[:, None] > token[None, :]).astype(jnp.bfloat16)
    rank = jnp.dot(earlier, member.astype(jnp.bfloat16), preferred_element_type=jnp.float32)
    rank = jnp.where(member, rank, -1.0)
    half_width = gate_halves.shape[2]
    if halves_dev == 1:
        parity = lax.axis_index(("seq", "head")) % 2
        other_gate, other_up, other_down = from_partner(
            (gate_halves, up_halves, down_halves), ("seq", "head"), 0
        )
        first_side = parity == 0
        stack = lambda own, other: jnp.where(
            first_side, jnp.stack([own, other], 1), jnp.stack([other, own], 1)
        )
        gate_w, up_w, down_w = (
            stack(gate_halves, other_gate),
            stack(up_halves, other_up),
            stack(down_halves, other_down),
        )
        items_dev = 1
    else:
        items_dev = halves_dev // 2
        gate_w = gate_halves.reshape(items_dev, 2, feature_width, half_width)
        up_w = up_halves.reshape(items_dev, 2, feature_width, half_width)
        down_w = down_halves.reshape(items_dev, 2, half_width, feature_width)
    slot_count = experts * capacity // (devices * items_dev)
    f32 = jnp.float32
    exchange = functools.partial(
        lax.all_to_all, axis_name=DEVICES, split_axis=0, concat_axis=0, tiled=True
    )
    moe_grad = out_grad.astype(f32)
    for item in range(items_dev):
        slot = (
            jnp.arange(devices)[:, None] * (items_dev * slot_count)
            + item * slot_count
            + jnp.arange(slot_count)[None, :]
        ).reshape(-1)
        slot_expert = (slot // capacity).astype(jnp.int32)
        pick = (expert_ids[:, None] == slot_expert[None, :]).astype(f32)
        slot_rank = jnp.dot(rank.astype(jnp.bfloat16), pick.astype(jnp.bfloat16), preferred_element_type=f32)
        here = slot_rank == (slot % capacity).astype(f32)[None, :]
        slot_gate = jnp.where(here, jnp.dot(gate_of, pick, precision=highest), 0.0)
        take = here.T.astype(jnp.bfloat16)
        send_input = jnp.dot(take, moe_input, preferred_element_type=jnp.bfloat16)
        send_grad = jnp.dot(take, out_grad, preferred_element_type=jnp.bfloat16)
        recv_input = exchange(send_input)
        recv_grad = exchange(send_grad)
        terms = swiglu_back(recv_input, recv_grad, gate_w[item], up_w[item], down_w[item])
        returned = exchange(terms)
        high, low = split_bf16(slot_gate)
        moe_grad = moe_grad + jnp.dot(high, returned, preferred_element_type=f32)
        moe_grad = moe_grad + jnp.dot(low, returned, preferred_element_type=f32)
    resid_grad = moe_grad.astype(jnp.bfloat16)
    inner_dev = out_proj.shape[0]
    heads_dev = skip_gain.shape[0]
    head_dim = inner_dev // heads_dev
    seq_rows, state_dim = b_proj.shape
    block_len = BLOCK
    block_count = seq_rows // block_len
    decay = log_decay.reshape(heads_dev, block_count, block_len)
    causal = jnp.arange(block_len)[:, None] >= jnp.arange(block_len)[None, :]
    within = jnp.einsum("hbr,tr->hbt", decay, causal.astype(f32), precision=highest)
    block_sum = within[:, :, -1]
    later_sum = [jnp.zeros((heads_dev,), f32)]
    for block in reversed(range(1, block_count)):
        later_sum.insert(0, later_sum[0] + block_sum[:, block])
    tail = jnp.stack(later_sum, 1)
    total = later_sum[0] + block_sum[:, 0]
    totals = lax.all_gather(total, "seq")
    seq_count, place = lax.axis_size("seq"), lax.axis_index("seq")
    between = jnp.zeros((heads_dev,), f32)
    carried = []
    for source in range(seq_count):
        carried.append(jnp.where(source > place, jnp.exp(between), 0.0))
        between = between + jnp.where(source > place, totals[source], 0.0)
    b_blocks = b_proj.reshape(block_count, block_len, state_dim)
    c_blocks = c_proj.reshape(block_count, block_len, state_dim)
    x_blocks = ssd_x.reshape(block_count, block_len, heads_dev, head_dim)
    scores = jnp.einsum("btn,bsn->bts", c_blocks, b_blocks, precision=highest)
    log_gap = within[:, :, :, None] - within[:, :, None, :]
    weights = jnp.where(causal, jnp.exp(jnp.where(causal, log_gap, 0.0)), 0.0) * scores[None]
    to_start = jnp.exp(within)
    to_end = jnp.exp(block_sum[:, :, None] - within)
    block_decay = jnp.exp(block_sum)
    ssd_grad = jnp.einsum(
        "td,kd->tk",
        lax.all_gather(resid_grad, "head", axis=0, tiled=True),
        out_proj,
        preferred_element_type=jnp.float32,
    )
    g_blocks = ssd_grad.reshape(block_count, block_len, heads_dev, head_dim)
    intra_x = jnp.einsum("hbts,bthp->bshp", weights, g_blocks, precision=highest)
    inner_prod = jnp.einsum("bthp,bshp->hbts", g_blocks, x_blocks, precision=highest)
    intra_b = jnp.einsum("hbts,btn->bsn", weights * inner_prod, c_blocks, precision=highest)
    block_state = jnp.einsum("hbt,bthp,btn->bhpn", to_start, g_blocks, c_blocks, precision=highest)

    carry = jnp.zeros((heads_dev, head_dim, state_dim), f32)
    after = []
    for block in reversed(range(block_count)):
        after.insert(0, carry)
        carry = block_decay[:, block, None, None] * carry + block_state[block]
    states = lax.all_gather(carry, "seq")
    incoming = sum(carried[s][:, None, None] * states[s] for s in range(seq_count))
    future = jnp.stack(after) + jnp.exp(tail).T[:, :, None, None] * incoming[None]
    cross_x = jnp.einsum("hbs,bsn,bhpn->bshp", to_end, b_blocks, future, precision=highest)
    grad_x = intra_x + cross_x + skip_gain[None, None, :, None] * g_blocks
    cross_b = jnp.einsum("hbs,bshp,bhpn->bsn", to_end, x_blocks, future, precision=highest)
    partial_b = (intra_b + cross_b).reshape(seq_rows, state_dim)
    parts = lax.all_to_all(partial_b, "head", split_axis=0, concat_axis=0, tiled=True)
    b_grad = jnp.sum(parts.reshape(lax.axis_size("head"), -1, state_dim), axis=0)
    return (resid_grad, grad_x.reshape(seq_rows, inner_dev), b_grad)


def solution(mesh):
    return jax.shard_map(
        shards,
        mesh=mesh,
        in_specs=(
            P(("seq", "head"), None),
            P(("seq", "head"), None),
            P(("seq", "head"), None),
            P(("seq", "head"), None),
            P(("seq", "head"), None, None),
            P(("seq", "head"), None, None),
            P(("seq", "head"), None, None),
            P("head", None),
            P("seq", "head"),
            P("seq", None),
            P("seq", None),
            P("head", "seq"),
            P("head"),
        ),
        out_specs=(P(("seq", "head"), None), P("seq", "head"), P(("seq", "head"), None)),
        check_vma=False,
    )
```

time: 488 us -> 389 us (0.80)
  blocking collectives: 95.2 us -> 15.4 us
  local copies, waits for them, and re-layouts: 77.5 us -> 20.5 us
  waiting for transfers between devices: 192 us -> 237 us
  other arithmetic: 33.4 us -> 4.5 us
  starting transfers between devices: 7.11 us -> 28.1 us
  Pallas kernels: 0 us -> 20.2 us
  matrix products: 61.9 us -> 47 us
    all_to_all x2 -> x7, waiting for transfers between devices: 111 us -> 196 us  [the longest x2 74 us: shards(): recv_input = exchange(send_input)]
    all_to_all x1 -> x0, blocking collectives: 79.7 us -> none  [shards(): lax.all_to_all(send_input, ('seq', 'head'), split_axis=0, concat_axis=0,...]
    reduce_scatter x1 -> x0, waiting for transfers between devices: 44.8 us -> none  [shards(): lax.psum_scatter(partial_b, 'head', scatter_dimension=0, tiled=True)]
    all_to_all x2 -> x7, starting transfers between devices: 6.62 us -> 27.8 us  [the longest x2 10.9 us: shards(): recv_input = exchange(send_input)]
    pallas_call x0 -> x2, Pallas kernels: none -> 20.2 us  [swiglu_back(): pl.pallas_call(expert_kernel, grid=(rows // tile,), in_specs=[row, row, p...]
    gather x3 -> x0, local copies, waits for them, and re-layouts: 17.8 us -> none  [the longest x1 8.39 us: shards(): input_rows = jnp.where(live_slot[:, None], moe_input[slot_token], zero_row)]
    transpose x2 -> x0, local copies, waits for them, and re-layouts: 15.9 us -> none  [the longest x1 7.97 us: shards(): gate_w = gate_halves.reshape(items_dev, 2, feature_width, half_width).tra...]
    dot_general x4 -> x14, matrix products: 28.4 us -> 16.3 us  [the longest x2 4.55 us: shards(): send_input = jnp.dot(take, moe_input, preferred_element_type=jnp.bfloat16)]
  transfers between devices with their start and end apart: 4 -> 8, of which waited for: 4 -> 8; matrix products, arithmetic and copies ran while one was open for 13% -> 10% of each run, Pallas kernels for 0% -> 5%
where the time goes in v1:
time: 389 us; the launch traced here: 388 us
  waiting for transfers between devices  237 us (61%)
  matrix products  47 us (12%)
  starting transfers between devices  28.1 us (7%)
  local copies, waits for them, and re-layouts  20.5 us (5%)
  Pallas kernels  20.2 us (5%)
  blocking collectives  15.4 us (4%)
  between operations  15.3 us (4%)
  other arithmetic  4.5 us (1%)
    all_to_all x2, waiting for transfers between devices, shards(): recv_input = exchange(send_input)  74 us
    all_to_all x2, waiting for transfers between devices, shards(): returned = exchange(terms)  64.5 us
    all_to_all x2, waiting for transfers between devices, shards(): recv_grad = exchange(send_grad)  54.4 us
    all_gather x1, waiting for transfers between devices, shards(): lax.all_gather(resid_grad, 'head', axis=0, tiled=True)  40.9 us
    pallas_call x2, Pallas kernels, swiglu_back(): pl.pallas_call(expert_kernel, grid=(rows // tile,), in_specs=[row, row, p...  20.2 us
    all_to_all x2, starting transfers between devices, shards(): recv_input = exchange(send_input)  10.9 us
    all_gather x1, blocking collectives, shards(): states = lax.all_gather(carry, 'seq')  8.93 us
  transfers between devices with their start and end apart: 8, of which 8 were waited for; matrix products, arithmetic and copies ran while one was open for 10% of the time, Pallas kernels for 5%

profile of v1, /device:TPU:0, one launch (start us, length us, event | category | flops | bytes accessed | tf_op | source)
XLA Modules:
  0.0 388.3 jit_solution(13579359157919456395)
XLA Ops:
  8.6 2.8 fusion.60
  11.4 7.3 %all-to-all-start = ((bf16[32,16,1536]{2,1,0:T(8,128)(2,1)}), bf16[32,16,1536]{2,1,0:T(8,128)(2,1)S(1)}, u32[]{:S(2)}, u32[]{:S(2)}) async-start(bf16[32,16,1536]{2,1,0:T(8,128)(2,1)} %bitcast.114), calls=%async_computation | async-start | bytes 3145728 | tf_op jit(solution)/shard_map/all_to_all | solution.py:137
  20.5 37.0 %all-to-all-done = bf16[32,16,1536]{2,1,0:T(8,128)(2,1)S(1)} async-done(((bf16[32,16,1536]{2,1,0:T(8,128)(2,1)}), bf16[32,16,1536]{2,1,0:T(8,128)(2,1)S(1)}, u32[]{:S(2)}, u32[]{:S(2)}) %all-to-all-start) | async-done | bytes 1572896 | tf_op jit(solution)/shard_map/all_to_all | solution.py:137
  57.5 3.5 all-to-all-start.1
  65.9 34.1 %all-to-all-done.1 = bf16[32,16,1536]{2,1,0:T(8,128)(2,1)} async-done(((bf16[32,16,1536]{2,1,0:T(8,128)(2,1)}), bf16[32,16,1536]{2,1,0:T(8,128)(2,1)}, u32[]{:S(2)}, u32[]{:S(2)}) %all-to-all-start.1) | async-done | bytes 1572896 | tf_op jit(solution)/shard_map/all_to_all | solution.py:138
  99.9 3.6 all-to-all-start.3
  105.3 37.0 %all-to-all-done.3 = bf16[32,16,1536]{2,1,0:T(8,128)(2,1)} async-done(((bf16[32,16,1536]{2,1,0:T(8,128)(2,1)}), bf16[32,16,1536]{2,1,0:T(8,128)(2,1)}, u32[]{:S(2)}, u32[]{:S(2)}) %all-to-all-start.3) | async-done | bytes 1572896 | tf_op jit(solution)/shard_map/all_to_all | solution.py:137
  142.3 3.4 all-to-all-start.4
  145.8 3.9 %fusion.57 = (bf16[2,256,1536]{2,1,0:T(8,128)(2,1)}, bf16[2,256,1536]{2,1,0:T(8,128)(2,1)}) fusion(bf16[4,256,1536]{2,1,0:T(8,128)(2,1)} %param.19), kind=kLoop, calls=%fused_computation.123 | loop fusion | bytes 6291456 | tf_op jit(solution)/shard_map/slice | solution.py:139
  150.7 2.8 fusion.58
  153.5 9.5 %shard_map.148 = bf16[512,1536]{1,0:T(8,128)(2,1)S(1)} custom-call(bf16[512,1536]{1,0:T(8,128)(2,1)S(1)} %bitcast.105, bf16[512,1536]{1,0:T(8,128)(2,1)} %bitcast.3.g_ref, bf16[2,1536,256]{2,1,0:T(8,128)(2,1)} %get-tuple-element.37.gate_ref, bf16[2,1536,256]{2,1,0:T(8,128)(2,1)} %get-tuple-element.24.up_ref, bf16[2,256,1536]{2,1,0:T(8,128)(2,1)} %get-tuple-element.22.down_ref), custom_call_target="tpu_custom_call" | custom-call | flops 4026531840 | bytes 9437184 | tf_op jit(solution)/shard_map/pallas_call | solution.py:40
  164.3 20.3 %all-to-all-done.4 = bf16[32,16,1536]{2,1,0:T(8,128)(2,1)} async-done(((bf16[32,16,1536]{2,1,0:T(8,128)(2,1)}), bf16[32,16,1536]{2,1,0:T(8,128)(2,1)}, u32[]{:S(2)}, u32[]{:S(2)}) %all-to-all-start.4) | async-done | bytes 1572896 | tf_op jit(solution)/shard_map/all_to_all | solution.py:138
  184.6 2.7 all-to-all-start.2
  187.3 10.7 %shard_map.149 = bf16[512,1536]{1,0:T(8,128)(2,1)} custom-call(bf16[512,1536]{1,0:T(8,128)(2,1)} %bitcast.7.x_ref, bf16[512,1536]{1,0:T(8,128)(2,1)} %bitcast.9.g_ref, bf16[2,1536,256]{2,1,0:T(8,128)(2,1)} %get-tuple-element.38.gate_ref, bf16[2,1536,256]{2,1,0:T(8,128)(2,1)} %get-tuple-element.23.up_ref, bf16[2,256,1536]{2,1,0:T(8,128)(2,1)} %get-tuple-element.21.down_ref), custom_call_target="tpu_custom_call" | custom-call | flops 4026531840 | bytes 9437184 | tf_op jit(solution)/shard_map/pallas_call | solution.py:40
  198.0 28.2 %all-to-all-done.2 = bf16[32,16,1536]{2,1,0:T(8,128)(2,1)S(1)} async-done(((bf16[32,16,1536]{2,1,0:T(8,128)(2,1)}), bf16[32,16,1536]{2,1,0:T(8,128)(2,1)S(1)}, u32[]{:S(2)}, u32[]{:S(2)}) %all-to-all-start.2) | async-done | bytes 1572896 | tf_op jit(solution)/shard_map/all_to_all | solution.py:140
  226.2 3.6 all-to-all-start.5
  232.2 36.4 %all-to-all-done.5 = bf16[32,16,1536]{2,1,0:T(8,128)(2,1)} async-done(((bf16[32,16,1536]{2,1,0:T(8,128)(2,1)}), bf16[32,16,1536]{2,1,0:T(8,128)(2,1)}, u32[]{:S(2)}, u32[]{:S(2)}) %all-to-all-start.5) | async-done | bytes 1572896 | tf_op jit(solution)/shard_map/all_to_all | solution.py:140
  268.6 1.9 convolution_add_fusion.1
  270.5 2.5 fusion.6
  279.4 6.5 %all-reduce = f32[24]{0:T(128)S(1)} all-reduce(f32[24]{0:T(128)S(1)} %get-tuple-element.14), channel_id=2, replica_groups=mesh['seq'=4,'head'=8] {'seq'}, use_global_device_ids=true, to_apply=%add | all-reduce | flops 24 | bytes 192
  287.3 3.0 fusion.65
  290.3 40.9 %all-gather.3.cloned.1.call-done = bf16[1024,1536]{1,0:T(8,128)(2,1)} async-done(((bf16[128,1536]{1,0:T(8,128)(2,1)}), bf16[1024,1536]{1,0:T(8,128)(2,1)}) %all-gather.3.cloned.1.call-update) | async-done | bytes 3145744 | tf_op jit(solution)/shard_map/all_gather | solution.py:178
  331.2 4.4 %fusion.64 = f32[1024,384]{0,1:T(8,128)} fusion(bf16[1024,1536]{1,0:T(8,128)(2,1)} %all-gather.3.cloned.1.call-done, bf16[384,1536]{1,0:T(8,128)(2,1)S(1)} %copy-done), kind=kOutput, calls=%fused_computation.130 | convolution fusion | flops 1207959552 | bytes 5898240 | tf_op jit(solution)/shard_map/td,kd->tk/dot_general | solution.py:176
  335.7 2.0 reshape.262
  339.9 8.9 %all_gather.12 = f32[4,6,64,128]{3,2,1,0:T(8,128)S(1)} all-gather(f32[1,6,64,128]{3,2,1,0:T(8,128)S(1)} %get-tuple-element.17), channel_id=1, replica_groups=mesh['seq'=4,'head'=8] {'seq'}, dimensions={0}, use_global_device_ids=true | all-gather | bytes 983040 | tf_op jit(solution)/shard_map/all_gather | solution.py:193
  348.8 7.5 %multiply_reduce_fusion = f32[4,256,256]{2,1,0:T(8,128)S(1)} fusion(f32[4,256,256]{2,1,0:T(8,128)S(1)} %copy-done.9, f32[6,4,256]{2,0,1:T(8,128)S(1)} %convolution_bitcast_fusion, pred[256,256]{1,0:T(8,128)(4,1)S(1)} %copy-done.18, f32[4,256,6,64]{1,0,3,2:T(4,128)S(1)} %copy-done.7, f32[4,256,6,64]{1,0,3,2:T(4,128)S(1)} %reshape.262), kind=kOutput, calls=%fused_computation | convolution fusion | flops 1217134592 | bytes 5332992 | tf_op jit(solution)/shard_map/bthp,bshp->hbts/dot_general | solution.py:184
  356.5 2.9 fusion.17
  359.4 2.7 convolution_add_fusion.4
  362.1 3.8 all-to-all-start.6
  365.9 2.9 fusion.22
  368.8 5.6 %fusion.8 = f32[4,256,6,64]{1,3,2,0:T(8,128)S(1)} fusion(f32[4,6,64,256]{3,2,1,0:T(8,128)S(1)} %fusion.22, f32[4,256,256]{2,1,0:T(8,128)S(1)} %copy-done.10, f32[6,4,256]{2,0,1:T(8,128)S(1)} %convolution_bitcast_fusion, pred[256,256]{1,0:T(8,128)(4,1)S(1)} %copy-done.19, f32[4,256,6,64]{1,0,3,2:T(4,128)S(1)} %reshape.262, f32[6]{0:T(128)S(1)} %copy-done.31, ...), kind=kOutput, calls=%fused_computation.15 | convolution fusion | flops 1215823872 | bytes 5881880 | tf_op jit(solution)/shard_map/hbts,bthp->bshp/dot_general | solution.py:183
  377.4 3.4 all-to-all-done.6
  (117 shorter events, 27.2 us)
Async XLA Ops:
  7.2 324.1 %copy-start = (bf16[384,1536]{1,0:T(8,128)(2,1)S(1)}, bf16[384,1536]{1,0:T(8,128)(2,1)}, u32[]{:S(2)}) copy-start(bf16[384,1536]{1,0:T(8,128)(2,1)} %param.20) | copy-start | bytes 3538948
  8.3 3.0 copy-start.33
  8.6 10.1 %copy-start.14 = (pred[128,512]{1,0:T(32,128)(4,1)}, pred[128,512]{1,0:T(32,128)(4,1)S(1)}, u32[]{:S(2)}) copy-start(pred[128,512]{1,0:T(32,128)(4,1)S(1)} %convolution_compare_fusion.1) | copy-start | bytes 196612
  11.4 7.3 %copy-start.3 = (bf16[128,1536]{1,0:T(8,128)(2,1)S(1)}, bf16[128,1536]{1,0:T(8,128)(2,1)}, u32[]{:S(2)}) copy-start(bf16[128,1536]{1,0:T(8,128)(2,1)} %param.14) | copy-start | bytes 1179652
  11.4 46.2 %all-to-all-start = ((bf16[32,16,1536]{2,1,0:T(8,128)(2,1)}), bf16[32,16,1536]{2,1,0:T(8,128)(2,1)S(1)}, u32[]{:S(2)}, u32[]{:S(2)}) async-start(bf16[32,16,1536]{2,1,0:T(8,128)(2,1)} %bitcast.114), calls=%async_computation | async-start | bytes 3145728 | tf_op jit(solution)/shard_map/all_to_all | solution.py:137
  57.5 6.6 %copy-start.8 = (bf16[128,1536]{1,0:T(8,128)(2,1)S(1)}, bf16[128,1536]{1,0:T(8,128)(2,1)}, u32[]{:S(2)}) copy-start(bf16[128,1536]{1,0:T(8,128)(2,1)} %param.13) | copy-start | bytes 1179652
  57.5 42.4 %all-to-all-start.1 = ((bf16[32,16,1536]{2,1,0:T(8,128)(2,1)}), bf16[32,16,1536]{2,1,0:T(8,128)(2,1)}, u32[]{:S(2)}, u32[]{:S(2)}) async-start(bf16[32,16,1536]{2,1,0:T(8,128)(2,1)} %bitcast.111), calls=%async_computation.1 | async-start | bytes 3145728 | tf_op jit(solution)/shard_map/all_to_all | solution.py:138
  99.9 3.6 copy-start.17
  99.9 42.4 %all-to-all-start.3 = ((bf16[32,16,1536]{2,1,0:T(8,128)(2,1)}), bf16[32,16,1536]{2,1,0:T(8,128)(2,1)}, u32[]{:S(2)}, u32[]{:S(2)}) async-start(bf16[32,16,1536]{2,1,0:T(8,128)(2,1)} %bitcast.113), calls=%async_computation.3 | async-start | bytes 3145728 | tf_op jit(solution)/shard_map/all_to_all | solution.py:137
  142.3 42.3 %all-to-all-start.4 = ((bf16[32,16,1536]{2,1,0:T(8,128)(2,1)}), bf16[32,16,1536]{2,1,0:T(8,128)(2,1)}, u32[]{:S(2)}, u32[]{:S(2)}) async-start(bf16[32,16,1536]{2,1,0:T(8,128)(2,1)} %bitcast.112), calls=%async_computation.4 | async-start | bytes 3145728 | tf_op jit(solution)/shard_map/all_to_all | solution.py:138
  145.8 3.9 %copy-start.4 = (bf16[4,1536,256]{2,1,0:T(8,128)(2,1)S(1)}, bf16[4,1536,256]{2,1,0:T(8,128)(2,1)}, u32[]{:S(2)}) copy-start(bf16[4,1536,256]{2,1,0:T(8,128)(2,1)} %param.18) | copy-start | bytes 9437188
  145.8 4.9 %copy-start.5 = (bf16[4,1536,256]{2,1,0:T(8,128)(2,1)S(1)}, bf16[4,1536,256]{2,1,0:T(8,128)(2,1)}, u32[]{:S(2)}) copy-start(bf16[4,1536,256]{2,1,0:T(8,128)(2,1)} %param.17) | copy-start | bytes 9437188
  184.6 41.5 %all-to-all-start.2 = ((bf16[32,16,1536]{2,1,0:T(8,128)(2,1)}), bf16[32,16,1536]{2,1,0:T(8,128)(2,1)S(1)}, u32[]{:S(2)}, u32[]{:S(2)}) async-start(bf16[32,16,1536]{2,1,0:T(8,128)(2,1)} %bitcast.106), calls=%async_computation.2 | async-start | bytes 3145728 | tf_op jit(solution)/shard_map/all_to_all | solution.py:140
  226.1 3.8 copy-start.20
  226.2 3.8 copy-start.23
  226.2 3.9 copy-start.15
  226.2 3.9 copy-start.22
  226.2 42.4 %all-to-all-start.5 = ((bf16[32,16,1536]{2,1,0:T(8,128)(2,1)}), bf16[32,16,1536]{2,1,0:T(8,128)(2,1)}, u32[]{:S(2)}, u32[]{:S(2)}) async-start(bf16[32,16,1536]{2,1,0:T(8,128)(2,1)} %bitcast.10), calls=%async_computation.5 | async-start | bytes 3145728 | tf_op jit(solution)/shard_map/all_to_all | solution.py:140
  229.7 101.5 %all-gather.3.cloned.1.call-start = ((), (), s32[]{:S(2)}) async-start(), calls=%async_computation.7 | async-start | bytes 3538944 | tf_op jit(solution)/shard_map/all_gather | solution.py:178
  275.6 11.7 %copy-start.2 = (f32[1024,128]{1,0:T(8,128)S(1)}, f32[1024,128]{1,0:T(8,128)}, u32[]{:S(2)}) copy-start(f32[1024,128]{1,0:T(8,128)} %param.23) | copy-start | bytes 1572868
  338.0 10.8 %copy-start.9 = (f32[4,256,256]{2,1,0:T(8,128)S(1)}, f32[4,256,256]{2,1,0:T(8,128)}, u32[]{:S(2)}) copy-start(f32[4,256,256]{2,1,0:T(8,128)} %fusion.65) | copy-start | bytes 3145732
  339.7 9.2 %copy-start.7 = (f32[4,256,6,64]{1,0,3,2:T(4,128)S(1)}, f32[4,256,6,64]{1,0,3,2:T(4,128)}, u32[]{:S(2)}) copy-start(f32[4,256,6,64]{1,0,3,2:T(4,128)} %reshape.267) | copy-start | bytes 4718596
  339.7 9.1 %copy-start.18 = (pred[256,256]{1,0:T(8,128)(4,1)S(1)}, pred[256,256]{1,0:T(8,128)(4,1)}, u32[]{:S(2)}) copy-start(pred[256,256]{1,0:T(8,128)(4,1)} %iota_compare_fusion) | copy-start | bytes 196612
  339.9 16.6 %copy-start.11 = (f32[1,6,64,128]{3,2,1,0:T(8,128)}, f32[1,6,64,128]{3,2,1,0:T(8,128)S(1)}, u32[]{:S(2)}) copy-start(f32[1,6,64,128]{3,2,1,0:T(8,128)S(1)} %get-tuple-element.19) | copy-start | bytes 589828
  339.9 16.6 %copy-start.12 = (f32[1,6,64,128]{3,2,1,0:T(8,128)}, f32[1,6,64,128]{3,2,1,0:T(8,128)S(1)}, u32[]{:S(2)}) copy-start(f32[1,6,64,128]{3,2,1,0:T(8,128)S(1)} %get-tuple-element.20) | copy-start | bytes 589828
  348.8 7.7 %copy-start.28 = (f32[4]{0:T(128)S(1)}, f32[4]{0:T(128)}, u32[]{:S(2)}) copy-start(f32[4]{0:T(128)} %pad.7.clone) | copy-start | bytes 52
  356.5 5.6 %copy-start.13 = (f32[6,64,128]{2,1,0:T(8,128)}, f32[6,64,128]{2,1,0:T(8,128)S(1)}, u32[]{:S(2)}) copy-start(f32[6,64,128]{2,1,0:T(8,128)S(1)} %fusion.31) | copy-start | bytes 589828
  359.4 6.5 %copy-start.29 = (f32[4]{0:T(128)S(1)}, f32[4]{0:T(128)}, u32[]{:S(2)}) copy-start(f32[4]{0:T(128)} %pad.7.clone) | copy-start | bytes 52
  362.1 18.7 %all-to-all-start.6 = ((f32[8,128,128]{2,1,0:T(8,128)}), f32[8,128,128]{2,1,0:T(8,128)S(1)}, u32[]{:S(2)}, u32[]{:S(2)}) async-start(f32[8,128,128]{2,1,0:T(8,128)} %bitcast.118), calls=%async_computation.6 | async-start | bytes 1048576 | tf_op jit(solution)/shard_map/all_to_all | solution.py:200
  365.9 2.9 copy-start.10
  365.9 2.9 copy-start.19
  365.9 2.9 copy-start.31
  (10 other events, 16.1 us)
Sparse Core Ops, SparseCore 0:
  273.2 57.9 all-gather.2
